TPU v7x, 32 devices: a whole 2x2x4 slice. The times are simulated.
32 devices in a mesh: sweep: 2 (over x), cell: 16 (over z, y, core).
Axes of the slice: x: 2, y: 2, z: 4, core: 2. Of those that a mesh axis runs over, the one named last changes fastest.
Arguments:
- populations: float32 [1024, 2, 2048], P(('sweep', 'cell')), parts along dimension 0, may hold values from 0.05 to 0.95
- coherences: float32 [1024, 2, 2048], P(('sweep', 'cell')), parts along dimension 0, may hold values from -0.4 to 0.4
- kernel: bfloat16 [2048, 2048], P('cell'), may hold values from 0 to 0.053710938
- velocity: float32 [2048], replicated, may hold values from 0.2 to 1
- heading: int32 [2048], replicated, may hold values from 0 to 1
- wall_flags: int32 [512], P('cell'), may hold values 0 or 1
- detune: float32 [4096], P('sweep'), parts along dimension 0, may hold values from -2 to 2
Outputs:
- populations_out: float32 [1024, 2, 2048], P(('sweep', 'cell')), parts along dimension 0
- coherences_out: float32 [1024, 2, 2048], P(('sweep', 'cell')), parts along dimension 0
There are 2 independent parts, one for each index of `sweep`. A program takes and returns all parts, laid end to end along the dimension named above; an argument that names none is the same for every part. Nothing has to cross between parts.
Inputs may be any that keep to these rules, and one draw needn't show every extreme that they name: `heading`: 1: the momentum moves toward higher cell indices; 0: toward lower ones. `wall_flags`: 1 marks an absorbing cell.
All inputs are finite; a program needn't handle non-finite values. No bound on the sum of `wall_flags` on one device may be relied on, other than what follows from the above.
Results may differ from a plain program's by a relative error of at most 0.0003.
Values may be sent and summed in bfloat16 or wider, within the bound.
A program may use at most 64 MiB of HBM per device.

v0:
```python
import functools

import jax
import jax.numpy as jnp
from jax import lax
from jax.experimental import pallas as pl
from jax.experimental.pallas import tpu as pltpu
from jax.sharding import PartitionSpec as P

STEPS = 4
TIME_STEP = 0.5
ABSORPTION = 1.0
LANES = 128
EDGE = 4
FORWARD = (-2.0, 15.0, -60.0, 20.0, 30.0, -3.0, 0.0)
BACKWARD = (0.0, 3.0, -30.0, -20.0, 60.0, -15.0, 2.0)
CHUNKS = 4
BLOCKS = 4


def fused(n, pop_ref, coh_ref, shard_ref, coef_ref, wall_ref, out_ref,
          kern, kern_t, dens, pred, s_dens, s_pred, e_dens, e_pred, gain, loss,
          halo_out, halo_in, ring_send, ring_recv, sib_send, sib_recv,
          halo_send, halo_recv, local_sem):
    cells = pop_ref.shape[0]
    momenta = shard_ref.shape[1]
    rows = shard_ref.shape[0]
    tiles = momenta // LANES
    width = momenta // CHUNKS
    chips = n // 2
    half = chips // 2
    first = 8
    last = first + cells

    me = lax.axis_index("cell")
    core = me % 2
    chip = me // 2
    sibling = chip * 2 + 1 - core
    odd = chip % 2
    spot = (1 - odd) * (chip // 2) + odd * (chips - 1 - chip // 2)

    def device_at(position):
        late = position // half
        at = (1 - late) * (2 * position) + late * (2 * (chips - 1 - position) + 1)
        return at * 2 + core

    right = device_at((spot + 1) % chips)
    left = device_at((spot + chips - 1) % chips)

    barrier = pltpu.get_barrier_semaphore()
    for other in (right, left, sibling, (me + 1) % n, (me + n - 1) % n):
        pl.semaphore_signal(barrier, inc=1, device_id={"cell": other})
    pl.semaphore_wait(barrier, 5)

    def place(device, chunk):
        return kern.at[pl.ds(pl.multiple_of(device * rows, rows), rows),
                       pl.ds(chunk * width, width)]

    def ring_copy(step, chunk, source):
        rightward = chunk < CHUNKS // 2
        position = (spot + chips - step) % chips if rightward else (spot + step) % chips
        here = place(device_at(position), chunk)
        src = shard_ref.at[:, pl.ds(chunk * width, width)] if source else here
        return pltpu.make_async_remote_copy(
            src_ref=src, dst_ref=here,
            send_sem=ring_send.at[chunk, step], recv_sem=ring_recv.at[chunk, step],
            device_id={"cell": right if rightward else left})

    def ring_arrival(step, chunk):
        rightward = chunk < CHUNKS // 2
        position = (spot + 2 * chips - 1 - step) % chips if rightward else (spot + 1 + step) % chips
        here = place(device_at(position), chunk)
        return here, device_at(position)

    def sib_copy(step, chunk, device, source):
        here = place(device, chunk)
        src = shard_ref.at[:, pl.ds(chunk * width, width)] if source else here
        return pltpu.make_async_remote_copy(
            src_ref=src, dst_ref=here,
            send_sem=sib_send.at[chunk, step], recv_sem=sib_recv.at[chunk, step],
            device_id={"cell": sibling})

    def other_core(device):
        return device + 1 - 2 * core

    for chunk in (0, 2, 1, 3):
        ring_copy(0, chunk, True).start()
    for chunk in range(CHUNKS):
        sib_copy(0, chunk, me, True).start()
    own = [pltpu.make_async_copy(shard_ref.at[:, pl.ds(chunk * width, width)],
                                 place(me, chunk), local_sem.at[chunk]) for chunk in range(CHUNKS)]
    for copy in own:
        copy.start()

    zeros = jnp.zeros((8, LANES), jnp.float32)

    def halo_copy(slot, way):
        return pltpu.make_async_remote_copy(
            src_ref=halo_out.at[slot, way], dst_ref=halo_in.at[slot, way],
            send_sem=halo_send.at[slot, way], recv_sem=halo_recv.at[slot, way],
            device_id={"cell": me - 1 if way == 0 else me + 1})

    def send_halo(state, slot):
        for way, start in ((0, first), (1, last - EDGE)):
            for c in range(4):
                halo_out[slot, way, :, c * EDGE:(c + 1) * EDGE, :] = state[c, :, start:start + EDGE, :]

        @pl.when(me > 0)
        def _():
            halo_copy(slot, 0).start()

        @pl.when(me < n - 1)
        def _():
            halo_copy(slot, 1).start()

    def take_halo(state, slot):
        @pl.when(me > 0)
        def _():
            halo_copy(slot, 0).wait_send()
            halo_copy(slot, 1).wait_recv()
            for c in range(4):
                state[c, :, first - EDGE:first, :] = halo_in[slot, 1, :, c * EDGE:(c + 1) * EDGE, :]

        @pl.when(me < n - 1)
        def _():
            halo_copy(slot, 1).wait_send()
            halo_copy(slot, 0).wait_recv()
            for c in range(4):
                state[c, :, last:last + EDGE, :] = halo_in[slot, 0, :, c * EDGE:(c + 1) * EDGE, :]

    def keep(t, parts, state, s_ref, e_ref):
        lane = pl.ds(t * LANES, LANES)
        for c in range(4):
            state[c, t, first:last, :] = parts[c]
            s_ref[c * cells:(c + 1) * cells, lane] = parts[c].astype(jnp.bfloat16)
        for c in range(2):
            e_ref[c * cells:(c + 1) * cells, lane] = (1.0 - parts[c]).astype(jnp.bfloat16)

    for state in (dens, pred):
        for c in range(4):
            for t in range(tiles):
                state[c, t, 0:8, :] = zeros
                state[c, t, last:last + 8, :] = zeros
    for t in range(tiles):
        lane = slice(t * LANES, (t + 1) * LANES)
        keep(t, [ref[:, b, lane] for ref in (pop_ref, coh_ref) for b in range(2)],
             dens, s_dens, e_dens)
    send_halo(dens, 0)

    def flip_block(row, column):
        block = kern[pl.ds(row, LANES), pl.ds(column, LANES)]
        kern_t[pl.ds(column, LANES), pl.ds(row, LANES)] = block.T

    whole_tiles = rows % LANES == 0

    def flip(device, chunk):
        if whole_tiles:
            for r in range(rows // LANES):
                for k in range(width // LANES):
                    flip_block(pl.multiple_of(device * rows + r * LANES, LANES),
                               chunk * width + k * LANES)

    for chunk in range(CHUNKS):
        own[chunk].wait()
        flip(me, chunk)

    def gather(step, _):
        for chunk in (0, 2, 1, 3):
            _, device = ring_arrival(step, chunk)
            ring_copy(step, chunk, False).wait_recv()

            @pl.when(step < chips - 2)
            def _():
                ring_copy(step + 1, chunk, False).start()

            sib_copy(step + 1, chunk, device, False).start()
            flip(device, chunk)
        for chunk in (0, 2, 1, 3):
            rightward = chunk < CHUNKS // 2
            position = (spot + chips - step) % chips if rightward else (spot + step) % chips
            device = other_core(device_at(position))
            sib_copy(step, chunk, device, False).wait_recv()
            flip(device, chunk)
        return 0

    lax.fori_loop(0, chips - 1, gather, 0)
    for chunk in (0, 2, 1, 3):
        rightward = chunk < CHUNKS // 2
        position = (spot + 1) % chips if rightward else (spot + chips - 1) % chips
        device = other_core(device_at(position))
        sib_copy(chips - 1, chunk, device, False).wait_recv()
        flip(device, chunk)

    def drain(step, _):
        for chunk in range(CHUNKS):
            @pl.when(step < chips - 1)
            def _():
                ring_copy(step, chunk, False).wait_send()

            sib_copy(step, chunk, me, False).wait_send()
        return 0

    lax.fori_loop(0, chips, drain, 0)

    if not whole_tiles:
        def flip_rows(r, _):
            for k in range(tiles):
                flip_block(pl.multiple_of(r * LANES, LANES), k * LANES)
            return 0

        lax.fori_loop(0, tiles, flip_rows, 0)

    span = momenta // BLOCKS

    def products(block, s_ref, e_ref):
        columns = slice(block * span, (block + 1) * span)
        gain[:, columns] = jnp.dot(s_ref[...], kern_t[:, columns], preferred_element_type=jnp.float32)
        loss[:, columns] = jnp.dot(e_ref[...], kern[:, columns], preferred_element_type=jnp.float32)

    def advance(block, state, finish):
        absorb = wall_ref[...]
        for t in range(block * tiles // BLOCKS, (block + 1) * tiles // BLOCKS):
            lane = slice(t * LANES, (t + 1) * LANES)
            row = [coef_ref[t, d:d + 1, :] for d in range(8)]
            detune = row[7]
            here = [state[c, t, first:last, :] for c in range(4)]
            g = [gain[c * cells:(c + 1) * cells, lane] for c in range(4)]
            l = [loss[c * cells:(c + 1) * cells, lane] for c in range(2)]
            mean_hole = 1.0 - 0.5 * (here[0] + here[1])
            damping = 0.5 * (l[0] + l[1])
            scatter = [
                (1.0 - here[0]) * g[0] - here[0] * l[0],
                (1.0 - here[1]) * g[1] - here[1] * l[1],
                mean_hole * g[2] - damping * here[2] - detune * here[3],
                mean_hole * g[3] - damping * here[3] + detune * here[2],
            ]
            moved = []
            for c in range(4):
                total = row[3] * here[c]
                for d in (0, 1, 2, 4, 5, 6):
                    total = total + row[d] * state[c, t, first - 3 + d:last - 3 + d, :]
                moved.append(total + scatter[c] - absorb * here[c])
            finish(t, here, moved)

    def stage(state, s_ref, e_ref, slot, finish):
        for block in range(BLOCKS):
            products(block, s_ref, e_ref)
            if block == 1:
                take_halo(state, slot)
            if block >= 1:
                advance(block - 1, state, finish)
        advance(BLOCKS - 1, state, finish)

    def predict(t, here, rate):
        keep(t, [here[c] + TIME_STEP * rate[c] for c in range(4)], pred, s_pred, e_pred)

    def correct(t, here, rate):
        keep(t, [0.5 * (dens[c, t, first:last, :] + here[c] + TIME_STEP * rate[c]) for c in range(4)],
             dens, s_dens, e_dens)

    def step(count, _):
        stage(dens, s_dens, e_dens, 0, predict)
        send_halo(pred, 1)
        stage(pred, s_pred, e_pred, 1, correct)

        @pl.when(count < STEPS - 1)
        def _():
            send_halo(dens, 0)

        return 0

    lax.fori_loop(0, STEPS, step, 0)
    for c in range(4):
        for t in range(tiles):
            out_ref[c, :, t * LANES:(t + 1) * LANES] = dens[c, t, first:last, :]


def on_device(populations, coherences, kernel, velocity, heading, wall_flags, detune):
    n = lax.axis_size("cell")
    cells, _, momenta = populations.shape
    tiles = momenta // LANES
    chips = n // 2
    forward = heading > 0
    scale = -velocity / 60.0
    rows = [scale * jnp.where(forward, a, b) for a, b in zip(FORWARD, BACKWARD)] + [detune]
    coef = jnp.stack([row.reshape(tiles, LANES) for row in rows], axis=1)
    wall = jnp.broadcast_to(ABSORPTION * wall_flags.astype(jnp.float32)[:, None], (cells, LANES))
    f32, bf16 = jnp.float32, jnp.bfloat16
    vmem = pltpu.VMEM
    dma = pltpu.SemaphoreType.DMA
    out = pl.pallas_call(
        functools.partial(fused, n),
        out_shape=jax.ShapeDtypeStruct((4, cells, momenta), f32),
        in_specs=[pl.BlockSpec(memory_space=vmem)] * 5,
        out_specs=pl.BlockSpec(memory_space=vmem),
        scratch_shapes=[
            vmem((momenta, momenta), bf16),
            vmem((momenta, momenta), bf16),
            vmem((4, tiles, cells + 16, LANES), f32),
            vmem((4, tiles, cells + 16, LANES), f32),
            vmem((4 * cells, momenta), bf16),
            vmem((4 * cells, momenta), bf16),
            vmem((2 * cells, momenta), bf16),
            vmem((2 * cells, momenta), bf16),
            vmem((4 * cells, momenta), f32),
            vmem((2 * cells, momenta), f32),
            vmem((2, 2, tiles, 4 * EDGE, LANES), f32),
            vmem((2, 2, tiles, 4 * EDGE, LANES), f32),
            dma((CHUNKS, chips)), dma((CHUNKS, chips)),
            dma((CHUNKS, chips)), dma((CHUNKS, chips)),
            dma((2, 2)), dma((2, 2)), dma((CHUNKS,)),
        ],
        compiler_params=pltpu.CompilerParams(
            collective_id=0, has_side_effects=True, vmem_limit_bytes=48 * 2**20),
        cost_estimate=pl.CostEstimate(
            flops=2 * STEPS * 2 * 6 * cells * momenta * momenta,
            bytes_accessed=3 * 2**20, transcendentals=0),
    )(populations, coherences, kernel, coef, wall)
    out = jnp.swapaxes(out, 0, 1)
    return out[:, :2], out[:, 2:]


def solution(mesh):
    in_specs = (
        P(("sweep", "cell"), None, None),
        P(("sweep", "cell"), None, None),
        P("cell", None),
        P(),
        P(),
        P("cell"),
        P("sweep"),
    )
    out_specs = (P(("sweep", "cell"), None, None), P(("sweep", "cell"), None, None))
    return jax.shard_map(
        on_device, mesh=mesh, in_specs=in_specs, out_specs=out_specs, check_vma=False
    )
```

profile of v0, /device:TPU:1, one launch (start us, length us, event | category | flops | bytes accessed | tf_op | source)
XLA Modules:
  0.0 107.5 jit_solution(1951587950227762444)
XLA Ops:
  0.6 0.0 copy-start.5
  0.6 0.6 copy-done.5
  1.3 0.7 select_multiply_fusion
  2.0 0.0 copy-start.3
  2.0 0.1 broadcast_in_dim.58.wall_ref
  2.1 0.6 copy-done.3
  2.7 0.0 copy-start.4
  2.7 0.7 copy-done.4
  3.4 0.1 stack.3.coef_ref
  3.5 0.0 copy-start
  3.5 1.0 copy-done
  4.6 0.0 copy-start.1
  4.6 1.0 copy-done.1
  5.6 0.0 copy-start.2
  5.6 1.0 copy-done.2
  6.7 98.3 %shard_map.86 = f32[4,32,2048]{2,1,0:T(8,128)S(1)} custom-call(f32[32,2,2048]{2,1,0:T(2,128)S(1)} %copy-done, f32[32,2,2048]{2,1,0:T(2,128)S(1)} %copy-done.1, bf16[128,2048]{1,0:T(8,128)(2,1)S(1)} %copy-done.2, f32[16,8,128]{2,1,0:T(8,128)S(1)} %stack.3.coef_ref, f32[32,128]{1,0:T(8,128)S(1)} %broadcast_in_dim.58.wall_ref), custom_call_target="tpu_custom_call" | custom-call | flops 12884901888 | bytes 3145728 | tf_op jit(solution)/shard_map/pallas_call | solution.py:291
  105.0 0.1 fusion
  105.1 1.2 %copy.10 = f32[32,2,2048]{2,1,0:T(2,128)} copy(f32[32,2,2048]{2,0,1:T(8,128)S(1)} %get-tuple-element.6) | data formatting | bytes 1048576
  106.3 1.2 %copy.9 = f32[32,2,2048]{2,1,0:T(2,128)} copy(f32[32,2,2048]{2,0,1:T(8,128)S(1)} %get-tuple-element.7) | data formatting | bytes 1048576
  (2 shorter events, 0.0 us)
Async XLA Ops:
  0.6 0.7 copy-start.5
  2.0 0.7 copy-start.3
  2.7 0.7 copy-start.4
  3.5 1.0 copy-start
  4.6 1.0 copy-start.1
  5.6 1.0 copy-start.2
where the time goes:
time: 108 us; the launch traced here: 107 us
  Pallas kernels  98.3 us (91%)
  local copies, waits for them, and re-layouts  7.73 us (7%)
    pallas_call x1, Pallas kernels, on_device(): pl.pallas_call(functools.partial(fused, n), out_shape=jax.ShapeDtypeStruc...  98.3 us
    unnamed x14, local copies, waits for them, and re-layouts  7.48 us

commit v1 on v0

v1 whole, which is shorter than its diff:
```python
import functools

import jax
import jax.numpy as jnp
from jax import lax
from jax.experimental import pallas as pl
from jax.experimental.pallas import tpu as pltpu
from jax.sharding import PartitionSpec as P

STEPS = 4
TIME_STEP = 0.5
ABSORPTION = 1.0
LANES = 128
EDGE = 3
PARTS = 2
FORWARD = (-2.0, 15.0, -60.0, 20.0, 30.0, -3.0, 0.0)
BACKWARD = (0.0, 3.0, -30.0, -20.0, 60.0, -15.0, 2.0)
CHUNKS = 8
RING = 6
CROSS = 2
BLOCKS = 4


def fused(n, pop_hbm, coh_hbm, shard_ref, coef_hbm, wall_hbm, out_ref,
          pop_ref, coh_ref, coef_ref, wall_ref, kern, kern_t, dens, pred, s_dens, s_pred, e_dens, e_pred, gain, loss,
          halo_out, halo_in, ring_send, ring_recv, sib_send, sib_recv, cross_send, cross_recv,
          halo_send, halo_recv, local_sem):
    cells = pop_ref.shape[0]
    momenta = shard_ref.shape[1]
    rows = shard_ref.shape[0]
    tiles = momenta // LANES
    width = momenta // CHUNKS
    chips = n // 2
    half = chips // 2
    first = 8
    last = first + cells

    me = lax.axis_index("cell")
    sweep = lax.axis_index("sweep")
    parity = sweep % 2
    peer = {"sweep": sweep + 1 - 2 * parity, "cell": me}
    core = me % 2
    chip = me // 2
    sibling = chip * 2 + 1 - core
    odd = chip % 2
    spot = (1 - odd) * (chip // 2) + odd * (chips - 1 - chip // 2)

    def device_at(position):
        late = position // half
        at = (1 - late) * (2 * position) + late * (2 * (chips - 1 - position) + 1)
        return at * 2 + core

    right = device_at((spot + 1) % chips)
    left = device_at((spot + chips - 1) % chips)

    barrier = pltpu.get_barrier_semaphore()
    for other in (right, left, sibling, (me + 1) % n, (me + n - 1) % n):
        pl.semaphore_signal(barrier, inc=1, device_id={"cell": other})
    pl.semaphore_signal(barrier, inc=1, device_id=peer)
    pl.semaphore_wait(barrier, 6)

    def columns_of(role):
        chunk = role + parity * (CHUNKS - 1 - 2 * role)
        return pl.multiple_of(chunk * width, width)

    def place(device, role):
        return kern.at[pl.ds(pl.multiple_of(device * rows, rows), rows),
                       pl.ds(columns_of(role), width)]

    def source(distance, role):
        rightward = role % 2 == 0 if role < RING else role % 2 == 1
        if rightward:
            return device_at((spot + chips - distance) % chips)
        return device_at((spot + distance) % chips)

    def piece(distance, role, own):
        here = place(source(distance, role), role)
        return (shard_ref.at[:, pl.ds(columns_of(role), width)] if own else here), here

    def ring_copy(step, role, own=False):
        src, here = piece(step, role, own)
        return pltpu.make_async_remote_copy(
            src_ref=src, dst_ref=here,
            send_sem=ring_send.at[role, step], recv_sem=ring_recv.at[role, step],
            device_id={"cell": right if role % 2 == 0 else left})

    def sib_copy(distance, role, own=False):
        src, here = piece(distance, role, own)
        return pltpu.make_async_remote_copy(
            src_ref=src, dst_ref=here,
            send_sem=sib_send.at[role, distance], recv_sem=sib_recv.at[role, distance],
            device_id={"cell": sibling})

    def cross_copy(step, role):
        src, here = piece(step + 1, role, False)
        return pltpu.make_async_remote_copy(
            src_ref=src, dst_ref=here,
            send_sem=cross_send.at[role, step], recv_sem=cross_recv.at[role, step],
            device_id=peer)

    def other_core(device):
        return device + 1 - 2 * core

    for role in range(RING):
        ring_copy(0, role, True).start()
    own = [pltpu.make_async_copy(shard_ref.at[:, pl.ds(columns_of(role), width)],
                                 place(me, role), local_sem.at[role]) for role in range(CHUNKS)]
    loads = [pltpu.make_async_copy(src, dst, local_sem.at[CHUNKS + i]) for i, (src, dst) in enumerate(
        ((pop_hbm, pop_ref), (coh_hbm, coh_ref), (coef_hbm, coef_ref), (wall_hbm, wall_ref)))]
    for copy in loads + own:
        copy.start()
    for role in range(CHUNKS):
        sib_copy(0, role, True).start()

    zeros = jnp.zeros((8, LANES), jnp.float32)

    pairs = tiles // 2
    depth = 4 * EDGE

    def halo_copy(slot, way, part):
        some = pl.ds(part * (pairs // PARTS), pairs // PARTS)
        return pltpu.make_async_remote_copy(
            src_ref=halo_out.at[slot, way, some], dst_ref=halo_in.at[slot, way, some],
            send_sem=halo_send.at[slot, way, part], recv_sem=halo_recv.at[slot, way, part],
            device_id={"cell": me - 1 if way == 0 else me + 1})

    def edge_rows(part):
        for t in range(part * (tiles // PARTS), (part + 1) * (tiles // PARTS)):
            for c in range(4):
                row = (t % 2) * depth + c * EDGE
                yield c, t, (t // 2, slice(row, row + EDGE), slice(None))

    def send_halo(state, slot, part):
        for way, start in ((0, first), (1, last - EDGE)):
            for c, t, spot_in in edge_rows(part):
                halo_out[(slot, way) + spot_in] = state[c, t, start:start + EDGE, :]

        @pl.when(me > 0)
        def _():
            halo_copy(slot, 0, part).start()

        @pl.when(me < n - 1)
        def _():
            halo_copy(slot, 1, part).start()

    def take_halo(state, slot, part):
        @pl.when(me > 0)
        def _():
            halo_copy(slot, 0, part).wait_send()
            halo_copy(slot, 1, part).wait_recv()
            for c, t, spot_in in edge_rows(part):
                state[c, t, first - EDGE:first, :] = halo_in[(slot, 1) + spot_in]

        @pl.when(me < n - 1)
        def _():
            halo_copy(slot, 1, part).wait_send()
            halo_copy(slot, 0, part).wait_recv()
            for c, t, spot_in in edge_rows(part):
                state[c, t, last:last + EDGE, :] = halo_in[(slot, 0) + spot_in]

    inner = cells - 16

    def of_cells(read, edge):
        if edge:
            return jnp.concatenate([read(0, 8), read(cells - 8, cells)], axis=0)
        return read(8, cells - 8)

    def row_range(c, edge):
        return slice(c * cells + inner, (c + 1) * cells) if edge else slice(c * cells, c * cells + inner)

    def keep(t, edge, parts, state, s_ref, e_ref):
        lane = pl.ds(t * LANES, LANES)
        for c in range(4):
            if edge:
                state[c, t, first:first + 8, :] = parts[c][:8]
                state[c, t, last - 8:last, :] = parts[c][8:]
            else:
                state[c, t, first + 8:last - 8, :] = parts[c]
            s_ref[row_range(c, edge), lane] = parts[c].astype(jnp.bfloat16)
        for c in range(2):
            e_ref[row_range(c, edge), lane] = (1.0 - parts[c]).astype(jnp.bfloat16)

    for state in (dens, pred):
        for c in range(4):
            for t in range(tiles):
                state[c, t, 0:8, :] = zeros
                state[c, t, last:last + 8, :] = zeros
    for copy in loads:
        copy.wait()
    for t in range(tiles):
        lane = slice(t * LANES, (t + 1) * LANES)
        for edge in (False, True):
            keep(t, edge, [of_cells(lambda i, j: ref[i:j, b, lane], edge)
                           for ref in (pop_ref, coh_ref) for b in range(2)],
                 dens, s_dens, e_dens)
    for part in range(PARTS):
        send_halo(dens, 0, part)

    def flip_block(row, column):
        block = kern[pl.ds(row, LANES), pl.ds(column, LANES)]
        kern_t[pl.ds(column, LANES), pl.ds(row, LANES)] = block.T

    whole_tiles = rows % LANES == 0

    def flip(device, role):
        if whole_tiles:
            for r in range(rows // LANES):
                for k in range(width // LANES):
                    flip_block(pl.multiple_of(device * rows + r * LANES, LANES),
                               pl.multiple_of(columns_of(role) + k * LANES, LANES))

    def from_sibling(distance, roles):
        for role in roles:
            sib_copy(distance, role).wait_recv()
            flip(other_core(source(distance, role)), role)

    ring_roles, cross_roles = range(RING), range(RING, CHUNKS)

    for role in range(CHUNKS):
        own[role].wait()
        flip(me, role)

    def gather(step, _):
        for role in ring_roles:
            ring_copy(step, role).wait_recv()

            @pl.when(step < chips - 2)
            def _():
                ring_copy(step + 1, role).start()

            if role < CROSS:
                cross_copy(step, role).start()
            sib_copy(step + 1, role).start()

        @pl.when(step > 0)
        def _():
            for role in cross_roles:
                cross_copy(step - 1, CHUNKS - 1 - role).wait_recv()
                sib_copy(step, role).start()

        for role in ring_roles:
            flip(source(step + 1, role), role)
        from_sibling(step, ring_roles)

        @pl.when(step > 0)
        def _():
            for role in cross_roles:
                flip(source(step, role), role)
            from_sibling(step - 1, cross_roles)

        return 0

    lax.fori_loop(0, chips - 1, gather, 0)
    for role in cross_roles:
        cross_copy(chips - 2, CHUNKS - 1 - role).wait_recv()
        sib_copy(chips - 1, role).start()
        flip(source(chips - 1, role), role)
    from_sibling(chips - 1, ring_roles)
    from_sibling(chips - 2, cross_roles)
    from_sibling(chips - 1, cross_roles)

    def drain(step, _):
        for role in range(CHUNKS):
            sib_copy(step, role).wait_send()

        @pl.when(step < chips - 1)
        def _():
            for role in ring_roles:
                ring_copy(step, role).wait_send()
            for role in range(CROSS):
                cross_copy(step, role).wait_send()

        return 0

    lax.fori_loop(0, chips, drain, 0)

    if not whole_tiles:
        def flip_rows(r, _):
            for k in range(tiles):
                flip_block(pl.multiple_of(r * LANES, LANES), k * LANES)
            return 0

        lax.fori_loop(0, tiles, flip_rows, 0)

    span = momenta // BLOCKS

    def products(block, s_ref, e_ref):
        columns = slice(block * span, (block + 1) * span)
        gain[:, columns] = jnp.dot(s_ref[...], kern_t[:, columns], preferred_element_type=jnp.float32)
        loss[:, columns] = jnp.dot(e_ref[...], kern[:, columns], preferred_element_type=jnp.float32)

    def shifted(state, c, t, d, edge):
        return of_cells(lambda i, j: state[c, t, first + i + d:first + j + d, :], edge)

    def advance(block, state, edge, finish):
        absorb = of_cells(lambda i, j: wall_ref[i:j, :], edge)
        for t in range(block * tiles // BLOCKS, (block + 1) * tiles // BLOCKS):
            lane = slice(t * LANES, (t + 1) * LANES)
            row = [coef_ref[t, d:d + 1, :] for d in range(8)]
            detune = row[7]
            here = [shifted(state, c, t, 0, edge) for c in range(4)]
            g = [gain[row_range(c, edge), lane] for c in range(4)]
            l = [loss[row_range(c, edge), lane] for c in range(2)]
            mean_hole = 1.0 - 0.5 * (here[0] + here[1])
            damping = 0.5 * (l[0] + l[1])
            scatter = [
                (1.0 - here[0]) * g[0] - here[0] * l[0],
                (1.0 - here[1]) * g[1] - here[1] * l[1],
                mean_hole * g[2] - damping * here[2] - detune * here[3],
                mean_hole * g[3] - damping * here[3] + detune * here[2],
            ]
            moved = []
            for c in range(4):
                total = row[3] * here[c]
                for d in (0, 1, 2, 4, 5, 6):
                    total = total + row[d] * shifted(state, c, t, d - 3, edge)
                moved.append(total + scatter[c] - absorb * here[c])
            finish(t, edge, here, moved)

    def stage(state, s_ref, e_ref, slot, finish, send):
        for block in range(BLOCKS):
            products(block, s_ref, e_ref)
            if block >= 1:
                advance(block - 1, state, False, finish)
        advance(BLOCKS - 1, state, False, finish)
        for part in range(PARTS):
            take_halo(state, slot, part)
            for block in range(part * BLOCKS // PARTS, (part + 1) * BLOCKS // PARTS):
                advance(block, state, True, finish)
            send(part)

    def predict(t, edge, here, rate):
        keep(t, edge, [here[c] + TIME_STEP * rate[c] for c in range(4)], pred, s_pred, e_pred)

    def correct(t, edge, here, rate):
        keep(t, edge, [0.5 * (shifted(dens, c, t, 0, edge) + here[c] + TIME_STEP * rate[c])
                       for c in range(4)], dens, s_dens, e_dens)

    def step(count, _):
        def send_density(part):
            @pl.when(count < STEPS - 1)
            def _():
                send_halo(dens, 0, part)

        stage(dens, s_dens, e_dens, 0, predict, lambda part: send_halo(pred, 1, part))
        stage(pred, s_pred, e_pred, 1, correct, send_density)
        return 0

    lax.fori_loop(0, STEPS, step, 0)
    for c in range(4):
        for t in range(tiles):
            out_ref[c, :, t * LANES:(t + 1) * LANES] = dens[c, t, first:last, :]


def on_device(populations, coherences, kernel, velocity, heading, wall_flags, detune):
    n = lax.axis_size("cell")
    cells, _, momenta = populations.shape
    tiles = momenta // LANES
    chips = n // 2
    forward = heading > 0
    scale = -velocity / 60.0
    rows = [scale * jnp.where(forward, a, b) for a, b in zip(FORWARD, BACKWARD)] + [detune]
    coef = jnp.stack([row.reshape(tiles, LANES) for row in rows], axis=1)
    wall = jnp.broadcast_to(ABSORPTION * wall_flags.astype(jnp.float32)[:, None], (cells, LANES))
    f32, bf16 = jnp.float32, jnp.bfloat16
    vmem = pltpu.VMEM
    dma = pltpu.SemaphoreType.DMA
    out = pl.pallas_call(
        functools.partial(fused, n),
        out_shape=jax.ShapeDtypeStruct((4, cells, momenta), f32),
        in_specs=[pl.BlockSpec(memory_space=pltpu.HBM)] * 5,
        out_specs=pl.BlockSpec(memory_space=vmem),
        scratch_shapes=[
            vmem(populations.shape, f32),
            vmem(coherences.shape, f32),
            vmem(coef.shape, f32),
            vmem(wall.shape, f32),
            vmem((momenta, momenta), bf16),
            vmem((momenta, momenta), bf16),
            vmem((4, tiles, cells + 16, LANES), f32),
            vmem((4, tiles, cells + 16, LANES), f32),
            vmem((4 * cells, momenta), bf16),
            vmem((4 * cells, momenta), bf16),
            vmem((2 * cells, momenta), bf16),
            vmem((2 * cells, momenta), bf16),
            vmem((4 * cells, momenta), f32),
            vmem((2 * cells, momenta), f32),
            vmem((2, 2, tiles // 2, 8 * EDGE, LANES), f32),
            vmem((2, 2, tiles // 2, 8 * EDGE, LANES), f32),
            dma((RING, chips)), dma((RING, chips)),
            dma((CHUNKS, chips)), dma((CHUNKS, chips)),
            dma((CROSS, chips)), dma((CROSS, chips)),
            dma((2, 2, PARTS)), dma((2, 2, PARTS)), dma((CHUNKS + 4,)),
        ],
        compiler_params=pltpu.CompilerParams(
            collective_id=0, has_side_effects=True, vmem_limit_bytes=48 * 2**20),
        cost_estimate=pl.CostEstimate(
            flops=2 * STEPS * 2 * 6 * cells * momenta * momenta,
            bytes_accessed=3 * 2**20, transcendentals=0),
    )(populations, coherences, kernel, coef, wall)
    out = jnp.swapaxes(out, 0, 1)
    return out[:, :2], out[:, 2:]


def solution(mesh):
    in_specs = (
        P(("sweep", "cell"), None, None),
        P(("sweep", "cell"), None, None),
        P("cell", None),
        P(),
        P(),
        P("cell"),
        P("sweep"),
    )
    out_specs = (P(("sweep", "cell"), None, None), P(("sweep", "cell"), None, None))
    return jax.shard_map(
        on_device, mesh=mesh, in_specs=in_specs, out_specs=out_specs, check_vma=False
    )
```

time: 108 us -> 83 us (0.77)
  Pallas kernels: 98.3 us -> 73.5 us
    pallas_call x1, Pallas kernels: 98.3 us -> 73.5 us  [on_device(): pl.pallas_call(functools.partial(fused, n), out_shape=jax.ShapeDtypeStruc...]
where the time goes in v1:
time: 83 us; the launch traced here: 82.6 us
  Pallas kernels  73.5 us (89%)
  local copies, waits for them, and re-layouts  7.73 us (9%)
    pallas_call x1, Pallas kernels, on_device(): pl.pallas_call(functools.partial(fused, n), out_shape=jax.ShapeDtypeStruc...  73.5 us
    unnamed x14, local copies, waits for them, and re-layouts  7.48 us

profile of v1, /device:TPU:1, one launch (start us, length us, event | category | flops | bytes accessed | tf_op | source)
XLA Modules:
  0.0 82.6 jit_solution(13606669346089449075)
XLA Ops:
  0.6 0.0 copy-start.5
  0.6 0.6 copy-done.5
  1.3 0.7 select_multiply_fusion
  2.0 0.0 copy-start.3
  2.0 0.1 broadcast_in_dim.58.wall_hbm
  2.1 0.6 copy-done.3
  2.7 0.0 copy-start.4
  2.7 0.7 copy-done.4
  3.4 0.1 stack.3.coef_hbm
  3.5 0.0 copy-start
  3.5 1.0 %copy-done = f32[32,2,2048]{2,1,0:T(2,128)S(1)} copy-done((f32[32,2,2048]{2,1,0:T(2,128)S(1)}, f32[32,2,2048]{2,1,0:T(2,128)}, u32[]{:S(2)}) %copy-start) | copy-done | bytes 524312
  4.6 0.0 copy-start.1
  4.6 1.0 %copy-done.1 = f32[32,2,2048]{2,1,0:T(2,128)S(1)} copy-done((f32[32,2,2048]{2,1,0:T(2,128)S(1)}, f32[32,2,2048]{2,1,0:T(2,128)}, u32[]{:S(2)}) %copy-start.1) | copy-done | bytes 524312
  5.6 0.0 copy-start.2
  5.6 1.0 %copy-done.2 = bf16[128,2048]{1,0:T(8,128)(2,1)S(1)} copy-done((bf16[128,2048]{1,0:T(8,128)(2,1)S(1)}, bf16[128,2048]{1,0:T(8,128)(2,1)}, u32[]{:S(2)}) %copy-start.2) | copy-done | bytes 524312
  6.7 73.5 %shard_map.86 = f32[4,32,2048]{2,1,0:T(8,128)S(1)} custom-call(f32[32,2,2048]{2,1,0:T(2,128)S(1)} %copy-done, f32[32,2,2048]{2,1,0:T(2,128)S(1)} %copy-done.1, bf16[128,2048]{1,0:T(8,128)(2,1)S(1)} %copy-done.2, f32[16,8,128]{2,1,0:T(8,128)S(1)} %stack.3.coef_hbm, f32[32,128]{1,0:T(8,128)S(1)} %broadcast_in_dim.58.wall_hbm), custom_call_target="tpu_custom_call" | custom-call | flops 12884901888 | bytes 3145728 | tf_op jit(solution)/shard_map/pallas_call | solution.py:368
  80.1 0.1 fusion
  80.2 1.2 %copy.10 = f32[32,2,2048]{2,1,0:T(2,128)} copy(f32[32,2,2048]{2,0,1:T(8,128)S(1)} %get-tuple-element.6) | data formatting | bytes 1048576
  81.4 1.2 %copy.9 = f32[32,2,2048]{2,1,0:T(2,128)} copy(f32[32,2,2048]{2,0,1:T(8,128)S(1)} %get-tuple-element.7) | data formatting | bytes 1048576
  (2 shorter events, 0.0 us)
Async XLA Ops:
  0.6 0.7 copy-start.5
  2.0 0.7 copy-start.3
  2.7 0.7 copy-start.4
  3.5 1.0 %copy-start = (f32[32,2,2048]{2,1,0:T(2,128)S(1)}, f32[32,2,2048]{2,1,0:T(2,128)}, u32[]{:S(2)}) copy-start(f32[32,2,2048]{2,1,0:T(2,128)} %pop_hbm.1) | copy-start | bytes 1572868
  4.6 1.0 %copy-start.1 = (f32[32,2,2048]{2,1,0:T(2,128)S(1)}, f32[32,2,2048]{2,1,0:T(2,128)}, u32[]{:S(2)}) copy-start(f32[32,2,2048]{2,1,0:T(2,128)} %coh_hbm.1) | copy-start | bytes 1572868
  5.6 1.0 %copy-start.2 = (bf16[128,2048]{1,0:T(8,128)(2,1)S(1)}, bf16[128,2048]{1,0:T(8,128)(2,1)}, u32[]{:S(2)}) copy-start(bf16[128,2048]{1,0:T(8,128)(2,1)} %shard_ref.1) | copy-start | bytes 1572868

commit v2 on v1

--- a/solution.py
+++ b/solution.py
@@ -18,7 +18,7 @@
 CHUNKS = 8
 RING = 6
 CROSS = 2
-BLOCKS = 4
+BLOCKS = 2
 
 
 def fused(n, pop_hbm, coh_hbm, shard_ref, coef_hbm, wall_hbm, out_ref,

time: 83 us -> 82.4 us (level)
  no operation moved by 1% of the time
where the time goes in v2:
time: 82.4 us; the launch traced here: 82 us
  Pallas kernels  72.9 us (88%)
  local copies, waits for them, and re-layouts  7.73 us (9%)
    pallas_call x1, Pallas kernels, on_device(): pl.pallas_call(functools.partial(fused, n), out_shape=jax.ShapeDtypeStruc...  72.9 us
    unnamed x14, local copies, waits for them, and re-layouts  7.48 us

profile of v2, /device:TPU:1, one launch (start us, length us, event | category | flops | bytes accessed | tf_op | source)
XLA Modules:
  0.0 82.0 jit_solution(10698248574886887109)
XLA Ops:
  0.6 0.0 copy-start.5
  0.6 0.6 copy-done.5
  1.3 0.7 select_multiply_fusion
  2.0 0.0 copy-start.3
  2.0 0.1 broadcast_in_dim.58.wall_hbm
  2.1 0.6 copy-done.3
  2.7 0.0 copy-start.4
  2.7 0.7 copy-done.4
  3.4 0.1 stack.3.coef_hbm
  3.5 0.0 copy-start
  3.5 1.0 %copy-done = f32[32,2,2048]{2,1,0:T(2,128)S(1)} copy-done((f32[32,2,2048]{2,1,0:T(2,128)S(1)}, f32[32,2,2048]{2,1,0:T(2,128)}, u32[]{:S(2)}) %copy-start) | copy-done | bytes 524312
  4.6 0.0 copy-start.1
  4.6 1.0 %copy-done.1 = f32[32,2,2048]{2,1,0:T(2,128)S(1)} copy-done((f32[32,2,2048]{2,1,0:T(2,128)S(1)}, f32[32,2,2048]{2,1,0:T(2,128)}, u32[]{:S(2)}) %copy-start.1) | copy-done | bytes 524312
  5.6 0.0 copy-start.2
  5.6 1.0 %copy-done.2 = bf16[128,2048]{1,0:T(8,128)(2,1)S(1)} copy-done((bf16[128,2048]{1,0:T(8,128)(2,1)S(1)}, bf16[128,2048]{1,0:T(8,128)(2,1)}, u32[]{:S(2)}) %copy-start.2) | copy-done | bytes 524312
  6.7 72.9 %shard_map.86 = f32[4,32,2048]{2,1,0:T(8,128)S(1)} custom-call(f32[32,2,2048]{2,1,0:T(2,128)S(1)} %copy-done, f32[32,2,2048]{2,1,0:T(2,128)S(1)} %copy-done.1, bf16[128,2048]{1,0:T(8,128)(2,1)S(1)} %copy-done.2, f32[16,8,128]{2,1,0:T(8,128)S(1)} %stack.3.coef_hbm, f32[32,128]{1,0:T(8,128)S(1)} %broadcast_in_dim.58.wall_hbm), custom_call_target="tpu_custom_call" | custom-call | flops 12884901888 | bytes 3145728 | tf_op jit(solution)/shard_map/pallas_call | solution.py:368
  79.5 0.1 fusion
  79.6 1.2 %copy.10 = f32[32,2,2048]{2,1,0:T(2,128)} copy(f32[32,2,2048]{2,0,1:T(8,128)S(1)} %get-tuple-element.6) | data formatting | bytes 1048576
  80.8 1.2 %copy.9 = f32[32,2,2048]{2,1,0:T(2,128)} copy(f32[32,2,2048]{2,0,1:T(8,128)S(1)} %get-tuple-element.7) | data formatting | bytes 1048576
  (2 shorter events, 0.0 us)
Async XLA Ops:
  0.6 0.7 copy-start.5
  2.0 0.7 copy-start.3
  2.7 0.7 copy-start.4
  3.5 1.0 %copy-start = (f32[32,2,2048]{2,1,0:T(2,128)S(1)}, f32[32,2,2048]{2,1,0:T(2,128)}, u32[]{:S(2)}) copy-start(f32[32,2,2048]{2,1,0:T(2,128)} %pop_hbm.1) | copy-start | bytes 1572868
  4.6 1.0 %copy-start.1 = (f32[32,2,2048]{2,1,0:T(2,128)S(1)}, f32[32,2,2048]{2,1,0:T(2,128)}, u32[]{:S(2)}) copy-start(f32[32,2,2048]{2,1,0:T(2,128)} %coh_hbm.1) | copy-start | bytes 1572868
  5.6 1.0 %copy-start.2 = (bf16[128,2048]{1,0:T(8,128)(2,1)S(1)}, bf16[128,2048]{1,0:T(8,128)(2,1)}, u32[]{:S(2)}) copy-start(bf16[128,2048]{1,0:T(8,128)(2,1)} %shard_ref.1) | copy-start | bytes 1572868
